TPU v7x, 256 devices: a whole 4x4x8 slice. The times are simulated.
256 devices in a mesh: band: 32 (over z, x_hi, core), fft: 8 (over x_lo, y).
Axes of the slice: x: 4 (x_hi: 2, x_lo: 2; x = x_hi * 2 + x_lo), y: 4, z: 8, core: 2. Of those that a mesh axis runs over, the one named last changes fastest.
Arguments:
- orbitals: float32 [32, 128, 128, 128], P('band', 'fft'), may hold values from -1.2 to 1.2
Outputs:
- own_exchange: float32 [32, 128, 128, 128], P('band', 'fft')
- source_exchange: float32 [4, 128, 128, 128], P(None, 'fft', 'band')
All inputs are finite; a program needn't handle non-finite values.
Results may differ from a plain program's by a relative error of at most 0.0003.
Values sent between devices are 32-bit elements; how exact they have to be, the bound alone decides.
A program may use at most 64 MiB of HBM per device.

v0:
```python
import jax
import jax.numpy as jnp
from jax import lax
from jax.sharding import PartitionSpec as P

ROUNDS = 4


cell_length = 51.3


def broadcast(value, axis, source):
    kept = jnp.where(lax.axis_index(axis) == source, value, 0).astype(value.dtype)
    return lax.psum(kept, axis)


def signed_square(indices, grid_size):
    signed = jnp.where(indices <= grid_size // 2, indices, indices - grid_size)
    return (signed * signed).astype(jnp.float32)


def coulomb_block(first, count, grid_size):
    whole = jnp.arange(grid_size, dtype=jnp.int32)
    block = first + jnp.arange(count, dtype=jnp.int32)
    total = (
        signed_square(whole, grid_size)[:, None, None]
        + signed_square(block, grid_size)[None, :, None]
        + signed_square(whole, grid_size)[None, None, :]
    )
    scale = cell_length * cell_length / jnp.pi
    return jnp.where(total > 0, scale / jnp.maximum(total, 1.0), 0.0)


def dft_tables(grid_size):
    indices = jnp.arange(grid_size, dtype=jnp.int32)
    phase = indices[:, None] * indices[None, :] % grid_size
    angle = phase.astype(jnp.float32) * (2.0 * jnp.pi / grid_size)
    return (jnp.cos(angle), jnp.sin(angle))


def transform_axis(real_part, imag_part, cosine, sine, form, inverse):
    highest = lax.Precision.HIGHEST
    cos_real = jnp.einsum(form, real_part, cosine, precision=highest)
    sin_real = jnp.einsum(form, real_part, sine, precision=highest)
    cos_imag = jnp.einsum(form, imag_part, cosine, precision=highest)
    sin_imag = jnp.einsum(form, imag_part, sine, precision=highest)
    if inverse:
        return (cos_real - sin_imag, cos_imag + sin_real)
    return (cos_real + sin_imag, cos_imag - sin_real)


def packed_potential(pack_real, pack_imag, kernel, cosine, sine):
    along_z = "qabn,nm->qabm"
    along_y = "qanc,nm->qamc"
    along_x = "qnbc,nm->qmbc"
    real_part, imag_part = transform_axis(pack_real, pack_imag, cosine, sine, along_z, False)
    real_part, imag_part = transform_axis(real_part, imag_part, cosine, sine, along_y, False)
    real_part, imag_part = (
        lax.all_to_all(real_part, "fft", split_axis=2, concat_axis=1, tiled=True),
        lax.all_to_all(imag_part, "fft", split_axis=2, concat_axis=1, tiled=True),
    )
    real_part, imag_part = transform_axis(real_part, imag_part, cosine, sine, along_x, False)
    real_part = real_part * kernel[None]
    imag_part = imag_part * kernel[None]
    real_part, imag_part = transform_axis(real_part, imag_part, cosine, sine, along_x, True)
    real_part, imag_part = (
        lax.all_to_all(real_part, "fft", split_axis=1, concat_axis=2, tiled=True),
        lax.all_to_all(imag_part, "fft", split_axis=1, concat_axis=2, tiled=True),
    )
    real_part, imag_part = transform_axis(real_part, imag_part, cosine, sine, along_y, True)
    real_part, imag_part = transform_axis(real_part, imag_part, cosine, sine, along_z, True)
    return (real_part, imag_part)


def local(orbitals):
    group_count = lax.axis_size("band")
    slab_count = lax.axis_size("fft")
    grid_size = orbitals.shape[2]
    block_width = grid_size // slab_count
    orbital = orbitals[0]
    stride = group_count // ROUNDS
    fetched = [broadcast(orbital, "band", turn * stride) for turn in range(ROUNDS)]
    first = lax.axis_index("fft") * block_width
    kernel = coulomb_block(first, block_width, grid_size) / float(grid_size) ** 3
    cosine, sine = dft_tables(grid_size)
    pack_count = ROUNDS // 2
    pack_real = jnp.stack([orbital * fetched[2 * turn] for turn in range(pack_count)])
    pack_imag = jnp.stack([orbital * fetched[2 * turn + 1] for turn in range(pack_count)])
    results = [
        packed_potential(
            pack_real[turn : turn + 1], pack_imag[turn : turn + 1], kernel, cosine, sine
        )
        for turn in range(pack_count)
    ]
    real_out = jnp.concatenate([item[0] for item in results], axis=0)
    imag_out = jnp.concatenate([item[1] for item in results], axis=0)
    potentials = []
    for turn in range(pack_count):
        potentials.append(real_out[turn])
        potentials.append(imag_out[turn])
    own = fetched[0] * potentials[0]
    for turn in range(1, ROUNDS):
        own = own + fetched[turn] * potentials[turn]
    term_list = [orbital * potentials[turn] for turn in range(ROUNDS)]
    source = lax.psum_scatter(jnp.stack(term_list), "band", scatter_dimension=2, tiled=True)
    return (own[None], source)


def solution(mesh):
    in_specs = (P("band", "fft", None, None),)
    out_specs = (P("band", "fft", None, None), P(None, "fft", "band", None))
    return jax.shard_map(local, mesh=mesh, in_specs=in_specs, out_specs=out_specs, check_vma=False)
```

profile of v0, /device:TPU:1, one launch (start us, length us, event | category | flops | bytes accessed | tf_op | source)
XLA Modules:
  0.0 627.0 jit_solution(14005825220271038095)
XLA Ops:
  7.2 3.5 bitcast_select_fusion.3
  10.8 287.0 %all-reduce.3.cloned.1.call-done = (f32[16,128,128]{2,1,0:T(8,128)}, f32[16,128,128]{2,1,0:T(8,128)}, f32[16,128,128]{2,1,0:T(8,128)}, f32[16,128,128]{2,1,0:T(8,128)}) async-done(((f32[16,128,128]{2,1,0:T(8,128)}, f32[16,128,128]{2,1,0:T(8,128)}, f32[16,128,128]{2,1,0:T(8,128)}, f32[16,128,128]{2,1,0:T(8,128)}), (f32[16,128,128]{2,1,0:T(8,128)}, f32[16,128,128]{2,1,0:T(8,128)}, f32[16,128,128]{2,1,0:T(8,128)}, ...) | async-done | bytes 4194320 | tf_op jit(solution)/shard_map/psum | solution.py:14
  297.9 2.5 fusion.22
  300.4 2.5 fusion.21
  304.2 1.3 fusion.56
  309.3 1.3 fusion.7
  310.6 1.6 copy.69
  312.2 1.6 copy.74
  313.8 4.5 all-to-all-start.4
  320.8 2.2 convolution_subtract_fusion.11
  323.0 2.2 convolution_add_fusion.11
  325.2 8.1 %all-to-all-done.4 = f32[1,16,128,128]{3,1,0,2:T(8,128)} async-done(((f32[1,16,128,128]{3,1,0,2:T(8,128)}), f32[1,16,128,128]{3,1,0,2:T(8,128)}, u32[]{:S(2)}, u32[]{:S(2)}) %all-to-all-start.4) | async-done | bytes 1048608 | tf_op jit(solution)/shard_map/all_to_all | solution.py:59
  333.3 3.6 all-to-all-start.5
  336.9 2.5 fusion.86
  339.4 1.3 fusion.15
  340.7 1.6 copy.45
  343.6 1.3 fusion.14
  344.9 1.6 copy.50
  346.5 1.3 copy.70
  347.8 4.0 all-to-all-done.5
  351.8 16.6 %all-to-all-start = ((f32[1,16,128,128]{3,1,0,2:T(8,128)}), f32[1,16,128,128]{3,1,0,2:T(8,128)}, u32[]{:S(2)}, u32[]{:S(2)}) async-start(f32[1,16,128,128]{3,1,0,2:T(8,128)} %copy.45), calls=%async_computation | async-start | bytes 2097152 | tf_op jit(solution)/shard_map/all_to_all | solution.py:59
  368.5 1.3 fusion.60
  369.9 1.3 fusion.54
  371.2 1.4 fusion.5
  372.6 2.7 fusion.4
  375.3 7.9 %all-to-all-done = f32[1,16,128,128]{3,1,0,2:T(8,128)} async-done(((f32[1,16,128,128]{3,1,0,2:T(8,128)}), f32[1,16,128,128]{3,1,0,2:T(8,128)}, u32[]{:S(2)}, u32[]{:S(2)}) %all-to-all-start) | async-done | bytes 1048608 | tf_op jit(solution)/shard_map/all_to_all | solution.py:59
  383.2 4.2 all-to-all-start.1
  390.0 1.6 copy.81
  391.6 1.3 copy.46
  393.0 2.3 fusion.52
  395.2 2.3 fusion.88
  397.5 4.9 all-to-all-done.1
  402.4 4.2 all-to-all-start.6
  407.9 1.6 copy.86
  409.5 1.3 copy.51
  412.2 1.4 fusion.13
  413.6 1.4 fusion.12
  415.1 6.5 %all-to-all-done.6 = f32[1,128,16,128]{3,2,0,1:T(8,128)} async-done(((f32[1,128,16,128]{3,2,0,1:T(8,128)}), f32[1,128,16,128]{3,2,0,1:T(8,128)}, u32[]{:S(2)}, u32[]{:S(2)}) %all-to-all-start.6) | async-done | bytes 1048608 | tf_op jit(solution)/shard_map/all_to_all | solution.py:67
  421.5 4.6 all-to-all-start.7
  428.8 1.6 copy.57
  431.7 1.3 fusion.10
  433.0 1.6 copy.62
  434.6 1.3 copy.82
  435.9 5.3 all-to-all-done.7
  441.2 4.3 all-to-all-start.3
  446.7 1.3 copy.87
  448.1 1.3 fusion.50
  449.4 1.3 fusion.1
  450.7 2.5 fusion
  453.2 7.2 %all-to-all-done.3 = f32[1,128,16,128]{3,2,0,1:T(8,128)} async-done(((f32[1,128,16,128]{3,2,0,1:T(8,128)}), f32[1,128,16,128]{3,2,0,1:T(8,128)}, u32[]{:S(2)}, u32[]{:S(2)}) %all-to-all-start.3) | async-done | bytes 1048608 | tf_op jit(solution)/shard_map/all_to_all | solution.py:68
  460.4 4.2 all-to-all-start.2
  466.1 2.3 copy.63
  469.6 2.2 convolution_add_fusion
  471.8 2.2 convolution_subtract_fusion
  474.1 5.5 all-to-all-done.2
  479.5 1.3 copy.58
  482.2 1.3 fusion.66
  484.8 1.4 fusion.8
  487.4 1.5 fusion.82
  490.2 2.4 bitcast_multiply_fusion.3
  493.0 4.4 copy.91
  499.3 4.3 add_bitcast_fusion
  503.6 114.7 %reduce-scatter.2.cloned.1.call-done = f32[4,16,4,128]{3,1,0,2:T(8,128)} async-done(((f32[4,16,128,128]{3,1,0,2:T(8,128)}), f32[4,16,4,128]{3,1,0,2:T(8,128)}) %reduce-scatter.2.cloned.1.call-update) | async-done | bytes 131088 | tf_op jit(solution)/shard_map/reduce_scatter | solution.py:105
  618.3 1.6 copy.92
  (70 shorter events, 29.4 us)
Async XLA Ops:
  7.2 290.7 %all-reduce.3.cloned.1.call-start = ((), (), s32[]{:S(2)}) async-start(), calls=%async_computation.10 | async-start | bytes 8388608 | tf_op jit(solution)/shard_map/psum | solution.py:14
  7.2 290.6 %copy-start = (f32[1,16,128,128]{3,2,1,0:T(8,128)S(1)}, f32[1,16,128,128]{3,2,1,0:T(8,128)}, u32[]{:S(2)}) copy-start(f32[1,16,128,128]{3,2,1,0:T(8,128)} %param.1) | copy-start | bytes 3145732
  297.8 5.1 copy-start.3
  300.4 5.1 copy-start.1
  309.3 9.0 %copy-start.5 = (f32[16,128,128]{2,1,0:T(8,128)S(1)}, f32[16,128,128]{2,1,0:T(8,128)}, u32[]{:S(2)}) copy-start(f32[16,128,128]{2,1,0:T(8,128)} %get-tuple-element.6) | copy-start | bytes 3145732
  312.2 7.3 %copy-start.7 = (f32[16,128,128]{2,1,0:T(8,128)S(1)}, f32[16,128,128]{2,1,0:T(8,128)}, u32[]{:S(2)}) copy-start(f32[16,128,128]{2,1,0:T(8,128)} %get-tuple-element.7) | copy-start | bytes 3145732
  313.8 19.5 %all-to-all-start.4 = ((f32[1,16,128,128]{3,1,0,2:T(8,128)}), f32[1,16,128,128]{3,1,0,2:T(8,128)}, u32[]{:S(2)}, u32[]{:S(2)}) async-start(f32[1,16,128,128]{3,1,0,2:T(8,128)} %copy.69), calls=%async_computation.4 | async-start | bytes 2097152 | tf_op jit(solution)/shard_map/all_to_all | solution.py:59
  323.0 16.4 %copy-start.10 = (f32[16,128,128]{2,1,0:T(8,128)S(1)}, f32[16,128,128]{2,1,0:T(8,128)}, u32[]{:S(2)}) copy-start(f32[16,128,128]{2,1,0:T(8,128)} %convolution_subtract_fusion.11) | copy-start | bytes 3145732
  333.3 18.6 %all-to-all-start.5 = ((f32[1,16,128,128]{3,1,0,2:T(8,128)}), f32[1,16,128,128]{3,1,0,2:T(8,128)S(1)}, u32[]{:S(2)}, u32[]{:S(2)}) async-start(f32[1,16,128,128]{3,1,0,2:T(8,128)} %copy.74), calls=%async_computation.5 | async-start | bytes 2097152 | tf_op jit(solution)/shard_map/all_to_all | solution.py:60
  339.4 4.2 copy-start.11
  347.8 23.4 %copy-start.18 = (f32[1,16,8,16,128]{4,1,2,3,0:T(8,128)}, f32[1,16,8,16,128]{4,1,2,3,0:T(8,128)S(1)}, u32[]{:S(2)}) copy-start(f32[1,16,8,16,128]{4,1,2,3,0:T(8,128)S(1)} %copy.70) | copy-start | bytes 3145732
  351.8 31.4 %all-to-all-start = ((f32[1,16,128,128]{3,1,0,2:T(8,128)}), f32[1,16,128,128]{3,1,0,2:T(8,128)}, u32[]{:S(2)}, u32[]{:S(2)}) async-start(f32[1,16,128,128]{3,1,0,2:T(8,128)} %copy.45), calls=%async_computation | async-start | bytes 2097152 | tf_op jit(solution)/shard_map/all_to_all | solution.py:59
  383.2 19.2 %all-to-all-start.1 = ((f32[1,16,128,128]{3,1,0,2:T(8,128)}), f32[1,16,128,128]{3,1,0,2:T(8,128)}, u32[]{:S(2)}, u32[]{:S(2)}) async-start(f32[1,16,128,128]{3,1,0,2:T(8,128)} %copy.50), calls=%async_computation.1 | async-start | bytes 2097152 | tf_op jit(solution)/shard_map/all_to_all | solution.py:60
  393.0 2.3 copy-start.16
  395.2 11.4 %copy-start.15 = (f32[128,16,128]{2,0,1:T(8,128)S(1)}, f32[128,16,128]{2,0,1:T(8,128)}, u32[]{:S(2)}) copy-start(f32[128,16,128]{2,0,1:T(8,128)} %fusion.52) | copy-start | bytes 3145732
  402.4 19.2 %all-to-all-start.6 = ((f32[1,128,16,128]{3,2,0,1:T(8,128)}), f32[1,128,16,128]{3,2,0,1:T(8,128)}, u32[]{:S(2)}, u32[]{:S(2)}) async-start(f32[1,128,16,128]{3,2,0,1:T(8,128)} %copy.81), calls=%async_computation.6 | async-start | bytes 2097152 | tf_op jit(solution)/shard_map/all_to_all | solution.py:67
  406.6 5.5 copy-start.19
  410.9 2.8 copy-start.17
  421.5 19.6 %all-to-all-start.7 = ((f32[1,128,16,128]{3,2,0,1:T(8,128)}), f32[1,128,16,128]{3,2,0,1:T(8,128)}, u32[]{:S(2)}, u32[]{:S(2)}) async-start(f32[1,128,16,128]{3,2,0,1:T(8,128)} %copy.86), calls=%async_computation.7 | async-start | bytes 2097152 | tf_op jit(solution)/shard_map/all_to_all | solution.py:68
  435.9 12.2 %copy-start.8 = (f32[1,8,16,16,128]{4,3,1,2,0:T(8,128)}, f32[1,8,16,16,128]{4,3,1,2,0:T(8,128)S(1)}, u32[]{:S(2)}) copy-start(f32[1,8,16,16,128]{4,3,1,2,0:T(8,128)S(1)} %copy.82) | copy-start | bytes 3145732
  441.2 19.2 %all-to-all-start.3 = ((f32[1,128,16,128]{3,2,0,1:T(8,128)}), f32[1,128,16,128]{3,2,0,1:T(8,128)}, u32[]{:S(2)}, u32[]{:S(2)}) async-start(f32[1,128,16,128]{3,2,0,1:T(8,128)} %copy.62), calls=%async_computation.3 | async-start | bytes 2097152 | tf_op jit(solution)/shard_map/all_to_all | solution.py:68
  460.4 19.2 %all-to-all-start.2 = ((f32[1,128,16,128]{3,2,0,1:T(8,128)}), f32[1,128,16,128]{3,2,0,1:T(8,128)}, u32[]{:S(2)}, u32[]{:S(2)}) async-start(f32[1,128,16,128]{3,2,0,1:T(8,128)} %copy.57), calls=%async_computation.2 | async-start | bytes 2097152 | tf_op jit(solution)/shard_map/all_to_all | solution.py:67
  464.6 153.7 %reduce-scatter.2.cloned.1.call-start = ((), (), s32[]{:S(2)}) async-start(), calls=%async_computation.9 | async-start | bytes 4325376 | tf_op jit(solution)/shard_map/reduce_scatter | solution.py:105
  471.8 10.3 %copy-start.9 = (f32[1,8,16,16,128]{4,3,1,2,0:T(8,128)S(1)}, f32[1,8,16,16,128]{4,3,1,2,0:T(8,128)}, u32[]{:S(2)}) copy-start(f32[1,8,16,16,128]{4,3,1,2,0:T(8,128)} %copy.63) | copy-start | bytes 3145732
  486.1 4.0 copy-start.12
  486.2 4.0 copy-start.13
  490.1 2.4 copy-start.14
  497.4 1.2 copy-start.2
  497.4 1.5 copy-start.4
  497.4 1.9 copy-start.6
Sparse Core Ops, SparseCore 0:
  11.4 286.3 all-reduce.2
  497.6 120.6 reduce-scatter.1
where the time goes:
time: 634 us; the launch traced here: 627 us
  waiting for transfers between devices  451 us (71%)
  matrix products  75.1 us (12%)
  starting transfers between devices  46.6 us (7%)
  local copies, waits for them, and re-layouts  31.1 us (5%)
  between operations  15 us (2%)
  other arithmetic  8.31 us (1%)
    psum x1, waiting for transfers between devices, broadcast(): return lax.psum(kept, axis)  287 us
    reduce_scatter x1, waiting for transfers between devices, local(): lax.psum_scatter(jnp.stack(term_list), 'band', scatter_dimension=2, tiled...  115 us
    all_to_all x2, starting transfers between devices, packed_potential(): lax.all_to_all(real_part, 'fft', split_axis=2, concat_axis=1, tiled=True)  21.1 us
    dot_general x12, matrix products, transform_axis(): sin_real = jnp.einsum(form, real_part, sine, precision=highest)  20 us
    dot_general x12, matrix products, transform_axis(): cos_real = jnp.einsum(form, real_part, cosine, precision=highest)  18.9 us
    dot_general x12, matrix products, transform_axis(): sin_imag = jnp.einsum(form, imag_part, sine, precision=highest)  18.7 us
    dot_general x12, matrix products, transform_axis(): cos_imag = jnp.einsum(form, imag_part, cosine, precision=highest)  17.5 us
    all_to_all x2, waiting for transfers between devices, packed_potential(): lax.all_to_all(real_part, 'fft', split_axis=2, concat_axis=1, tiled=True)  15.9 us
  transfers between devices with their start and end apart: 10, of which 10 were waited for; matrix products, arithmetic and copies ran while one was open for 12% of the time, Pallas kernels for 0%

commit v1 on v0

v1 whole, which is shorter than its diff:
```python
import functools

import jax
import jax.numpy as jnp
import ml_dtypes
import numpy as np
from jax import lax
from jax.experimental import pallas as pl
from jax.experimental.pallas import tpu as pltpu
from jax.sharding import PartitionSpec as P

N = 128
ROUNDS = 4
SLAB = 16
STEPS = 8
PACKS = 2
ZS = 8
CELL = 51.3
MESH = pl.DeviceIdType.MESH


def matrices():
    index = np.arange(N)
    angle = 2.0 * np.pi * (np.outer(index, index) % N) / N
    cosine, sine = np.cos(angle), np.sin(angle)
    forward = np.block([[cosine, -sine], [sine, cosine]])

    def split(matrix):
        high = matrix.astype(np.float32).astype(ml_dtypes.bfloat16)
        low = (matrix - high.astype(np.float64)).astype(np.float32).astype(ml_dtypes.bfloat16)
        return high, low

    def right(matrix):
        high, low = split(matrix)
        return np.concatenate([high, high, low], axis=0)

    def left(matrix):
        high, low = split(matrix)
        return np.concatenate([high, high, low], axis=1)

    return right(forward), left(forward.T), left(forward), right(forward.T)


def parts(value, axis):
    high = value.astype(jnp.bfloat16)
    low = (value - high.astype(jnp.float32)).astype(jnp.bfloat16)
    return jnp.concatenate([high, low, high], axis=axis)


def from_right(value, matrix):
    return jnp.dot(parts(value, 1), matrix, preferred_element_type=jnp.float32)


def from_left(matrix, value):
    return jnp.dot(matrix, parts(value, 0), preferred_element_type=jnp.float32)


def signed_square(index):
    signed = jnp.where(index <= N // 2, index, index - N)
    return (signed * signed).astype(jnp.float32)


def kernel(
    orb, right_fwd, left_fwd, left_inv, right_inv, own, out,
    srcs, send_a, recv_b, back, recv_c, terms, summed, gathered, coulomb, folded, folded_in, final, final_in,
    src_recv, src_send, a_recv, a_send, c_recv, c_send, t_recv, t_send, z_recv, z_send, x_sem, f_sem,
):
    band = lax.axis_index("band")
    me = lax.axis_index("fft")
    z = band // 4
    x_hi = lax.rem(band // 2, 2)
    core = lax.rem(band, 2)
    x_lo = me // 4
    y = lax.rem(me, 4)
    even = lax.rem(z, 2) == 0
    root = jnp.logical_and(jnp.logical_and(even, x_hi == 0), core == 0)
    lead = core == 0

    def device(z_at, x_hi_at, core_at):
        return {"band": z_at * 4 + x_hi_at * 2 + core_at, "fft": me}

    plus = device(lax.rem(z + 1, ZS), x_hi, core)
    minus = device(lax.rem(z + ZS - 1, ZS), x_hi, core)
    sibling = device(z, x_hi, 1 - core)
    across = device(z, 1 - x_hi, core)

    def peer_index(step):
        d_lo, d_y = step // 4, lax.rem(step, 4)
        return lax.rem(x_lo + d_lo, 2) * 4 + lax.rem(y + d_y, 4)

    barrier = pltpu.get_barrier_semaphore()

    def signal(target):
        pl.semaphore_signal(barrier, inc=1, device_id=target, device_id_type=MESH)

    for step in range(1, 8):
        signal({"band": band, "fft": peer_index(step)})
    for step in range(1, ZS):
        signal(device(lax.rem(z + step, ZS), x_hi, core))
    signal(sibling)
    signal(across)
    pl.semaphore_wait(barrier, 16)

    def round_of(slot):
        return lax.rem(z // 2 + slot, ROUNDS)

    def planes(j):
        return pl.ds(2 * j, 2)

    def remote(src, dst, send_sem, recv_sem, target):
        return pltpu.make_async_remote_copy(
            src_ref=src, dst_ref=dst, send_sem=send_sem, recv_sem=recv_sem, device_id=target, device_id_type=MESH
        )

    def pass_on(src, slot, j, kind, target):
        r = round_of(slot)
        remote(src, srcs.at[r, planes(j)], src_send.at[slot, kind], src_recv.at[r, j], target).start()

    @pl.when(root)
    def _():
        def body(j, carry):
            chunk = orb.at[planes(j)]
            pass_on(chunk, 0, j, 0, plus)
            pass_on(chunk, 0, j, 1, minus)
            pass_on(chunk, 0, j, 2, sibling)
            pass_on(chunk, 0, j, 3, across)
            return carry

        lax.fori_loop(0, STEPS, body, 0)

        def fill(j, carry):
            srcs[round_of(0), planes(j)] = orb[planes(j)]
            return carry

        lax.fori_loop(0, STEPS, fill, 0)

    def arrive(slot, j):
        r = round_of(slot)
        chunk = srcs.at[r, planes(j)]

        def take():
            pltpu.make_async_copy(chunk, chunk, src_recv.at[r, j]).wait()

            @pl.when(lead)
            def _():
                if slot in (0, 3):
                    pass_on(chunk, slot, j, 0, plus)
                if slot == 1:
                    pass_on(chunk, slot, j, 1, minus)
                if slot == 0:

                    @pl.when(even)
                    def _():
                        pass_on(chunk, slot, j, 1, minus)

                pass_on(chunk, slot, j, 2, sibling)

        if slot == 0:
            pl.when(jnp.logical_not(root))(take)
        else:
            take()

    def fill_coulomb(k, carry):
        row = lax.broadcasted_iota(jnp.int32, (N, N), 0)
        column = lax.broadcasted_iota(jnp.int32, (N, N), 1)
        middle = jnp.full((N, N), me * SLAB + k, jnp.int32)
        total = signed_square(row) + signed_square(middle) + signed_square(column)
        scale = CELL * CELL / np.pi / float(N) ** 3
        coulomb[k] = jnp.where(total > 0, scale / jnp.maximum(total, 1.0), 0.0)
        return carry

    lax.fori_loop(0, SLAB, fill_coulomb, 0)

    def forward(p, j):
        r_a, r_b = round_of(2 * p), round_of(2 * p + 1)
        rows = []
        for i in range(2):
            o = orb[2 * j + i]
            rows.append(jnp.concatenate([o * srcs[r_a, 2 * j + i], o * srcs[r_b, 2 * j + i]], axis=1))
        along_z = from_right(jnp.concatenate(rows, axis=0), right_fwd[...])
        real = jnp.concatenate([along_z[:N, :N], along_z[N:, :N]], axis=1)
        imag = jnp.concatenate([along_z[:N, N:], along_z[N:, N:]], axis=1)
        along_y = from_left(left_fwd[...], jnp.concatenate([real, imag], axis=0))
        for i in range(2):
            for part in range(2):
                send_a[p, 2 * j + i, part] = along_y[part * N : (part + 1) * N, i * N : (i + 1) * N]
        place = pl.ds(me * SLAB + 2 * j, 2)

        def block(f):
            return send_a.at[p, planes(j), :, pl.ds(pl.multiple_of(f * SLAB, SLAB), SLAB), :]

        for step in (5, 7, 6, 1, 3, 2, 4):
            f = peer_index(step)
            remote(
                block(f), recv_b.at[p, place], a_send.at[p], a_recv.at[p], {"band": band, "fft": f}
            ).start()
        pltpu.make_async_copy(block(me), recv_b.at[p, place], a_recv.at[p]).start()

    def first_steps(j, carry):
        arrive(0, j)
        arrive(1, j)
        forward(0, j)
        arrive(3, j)
        arrive(2, j)
        return carry

    def second_steps(j, carry):
        forward(1, j)
        return carry

    lax.fori_loop(0, STEPS, first_steps, 0)
    lax.fori_loop(0, STEPS, second_steps, 0)

    def middle(p):
        pltpu.make_async_copy(recv_b.at[p], recv_b.at[p], a_recv.at[p]).wait()
        flat_in = recv_b.at[p].reshape(N * 2 * SLAB, N)
        flat_out = back.at[p].reshape(N * 2 * SLAB, N)

        def rows(part, k):
            return pl.ds(part * SLAB + k, N, stride=2 * SLAB)

        def body(i, carry):
            blocks = [
                jnp.concatenate([flat_in[rows(part, 2 * i), :], flat_in[rows(part, 2 * i + 1), :]], axis=1)
                for part in range(2)
            ]
            spectrum = from_left(left_fwd[...], jnp.concatenate(blocks, axis=0))
            weight = jnp.concatenate([coulomb[2 * i], coulomb[2 * i + 1]], axis=1)
            spectrum = spectrum * jnp.concatenate([weight, weight], axis=0)
            result = from_left(left_inv[...], spectrum)
            for part in range(2):
                for n in range(2):
                    flat_out[rows(part, 2 * i + n), :] = result[part * N : (part + 1) * N, n * N : (n + 1) * N]
            return carry

        lax.fori_loop(0, SLAB // 2, body, 0)

        def give(j, carry):
            def place(ref):
                return ref.at[p, planes(j), :, pl.ds(pl.multiple_of(me * SLAB, SLAB), SLAB), :]

            for step in (5, 7, 6, 1, 3, 2, 4):
                f = peer_index(step)
                remote(
                    back.at[p, pl.ds(f * SLAB + 2 * j, 2)], place(recv_c), c_send.at[p], c_recv.at[p, j],
                    {"band": band, "fft": f},
                ).start()
            pltpu.make_async_copy(
                back.at[p, pl.ds(me * SLAB + 2 * j, 2)], place(recv_c), c_recv.at[p, j]
            ).start()
            return carry

        lax.fori_loop(0, STEPS, give, 0)

    for p in range(PACKS):
        middle(p)

    def inverse(p, j):
        chunk = recv_c.at[p, planes(j)]
        pltpu.make_async_copy(chunk, chunk, c_recv.at[p, j]).wait()
        parts_in = [
            jnp.concatenate([recv_c[p, 2 * j, part], recv_c[p, 2 * j + 1, part]], axis=1) for part in range(2)
        ]
        along_y = from_left(left_inv[...], jnp.concatenate(parts_in, axis=0))
        rows = [
            jnp.concatenate([along_y[:N, i * N : (i + 1) * N], along_y[N:, i * N : (i + 1) * N]], axis=1)
            for i in range(2)
        ]
        potential = from_right(jnp.concatenate(rows, axis=0), right_inv[...])
        r_a, r_b = round_of(2 * p), round_of(2 * p + 1)
        for i in range(2):
            pot_a = potential[i * N : (i + 1) * N, :N]
            pot_b = potential[i * N : (i + 1) * N, N:]
            share = srcs[r_a, 2 * j + i] * pot_a + srcs[r_b, 2 * j + i] * pot_b
            if p > 0:
                share = own[2 * j + i] + share
            own[2 * j + i] = share
            o = orb[2 * j + i]
            terms[p, j, i, 0] = o * pot_a
            terms[p, j, i, 1] = o * pot_b
        remote(
            terms.at[p, j, 1 - core], summed.at[p, j], t_send.at[p], t_recv.at[p, j], sibling
        ).start()

    def spread(p, j):
        chunk = summed.at[p, j]
        pltpu.make_async_copy(chunk, chunk, t_recv.at[p, j]).wait()
        summed[p, j] = summed[p, j] + terms[p, j, core]

        def rows(z_at):
            return summed.at[p, j, :, pl.ds(pl.multiple_of(z_at * 16, 16), 16), :]

        for step in (4, 3, 5, 2, 6, 1, 7):
            z_at = lax.rem(z + step, ZS)
            remote(
                rows(z_at), gathered.at[z, pl.ds(2 * p, 2), j], z_send.at[p], z_recv.at[0], device(z_at, x_hi, core)
            ).start()
        gathered[z, pl.ds(2 * p, 2), j] = summed[p, j, :, pl.ds(pl.multiple_of(z * 16, 16), 16), :]

    for p in range(PACKS):

        def step_body(j, carry):
            inverse(p, j)

            @pl.when(j > 0)
            def _():
                spread(p, j - 1)

            return carry

        lax.fori_loop(0, STEPS, step_body, 0)
        spread(p, STEPS - 1)

    pltpu.make_async_copy(gathered.at[pl.ds(0, 7)], gathered.at[pl.ds(0, 7)], z_recv.at[0]).wait()
    for r in range(ROUNDS):
        total = gathered[0, r]
        for z_at in range(1, ZS):
            total = total + gathered[z_at, (r - z_at // 2) % ROUNDS]
        folded[r] = total

    def half(x_hi_at):
        return pl.ds(pl.multiple_of(x_hi_at * 8, 8), 8)

    cross = remote(folded.at[:, :, half(1 - x_hi), :], folded_in, x_sem.at[0], x_sem.at[1], across)
    cross.start()
    cross.wait()
    final[...] = folded[:, :, half(x_hi), :] + folded_in[...]
    last = remote(final, final_in, f_sem.at[0], f_sem.at[1], sibling)
    last.start()
    last.wait()

    def write(j, carry):
        for r in range(ROUNDS):
            mine, theirs = final[r, j], final_in[r, j]
            out[r, 2 * j + core] = jnp.where(core == 0, mine[:4], mine[4:])
            out[r, 2 * j + 1 - core] = jnp.where(core == 0, theirs[:4], theirs[4:])
        return carry

    lax.fori_loop(0, STEPS, write, 0)

    def sent(ref, sem):
        pltpu.make_async_copy(ref, ref, sem).wait()

    for p in range(PACKS):
        sent(send_a.at[p, pl.ds(0, 14)], a_send.at[p])
        sent(back.at[p, pl.ds(0, 112)], c_send.at[p])
        sent(summed.at[p], t_send.at[p])
        sent(summed.at[p, pl.ds(0, 7)], z_send.at[p])

    @pl.when(lead)
    def _():
        for slot, kind in ((0, 0), (0, 2), (1, 1), (1, 2), (2, 2), (3, 0), (3, 2)):
            sent(srcs.at[slot], src_send.at[slot, kind])

        @pl.when(even)
        def _():
            sent(srcs.at[0], src_send.at[0, 1])

        @pl.when(root)
        def _():
            sent(srcs.at[0], src_send.at[0, 3])


def local(right_fwd, left_fwd, left_inv, right_inv, orbitals):
    f32 = jnp.float32
    dma = pltpu.SemaphoreType.DMA
    vmem = pl.BlockSpec(memory_space=pltpu.VMEM)
    own, source = pl.pallas_call(
        kernel,
        out_shape=(
            jax.ShapeDtypeStruct((SLAB, N, N), f32),
            jax.ShapeDtypeStruct((ROUNDS, SLAB, 4, N), f32),
        ),
        in_specs=[vmem] * 5,
        out_specs=(vmem, vmem),
        scratch_shapes=[
            pltpu.VMEM((ROUNDS, SLAB, N, N), f32),
            pltpu.VMEM((PACKS, SLAB, 2, N, N), f32),
            pltpu.VMEM((PACKS, N, 2, SLAB, N), f32),
            pltpu.VMEM((PACKS, N, 2, SLAB, N), f32),
            pltpu.VMEM((PACKS, SLAB, 2, N, N), f32),
            pltpu.VMEM((PACKS, STEPS, 2, 2, N, N), f32),
            pltpu.VMEM((PACKS, STEPS, 2, N, N), f32),
            pltpu.VMEM((ZS, ROUNDS, STEPS, 16, N), f32),
            pltpu.VMEM((SLAB, N, N), f32),
            pltpu.VMEM((ROUNDS, STEPS, 16, N), f32),
            pltpu.VMEM((ROUNDS, STEPS, 8, N), f32),
            pltpu.VMEM((ROUNDS, STEPS, 8, N), f32),
            pltpu.VMEM((ROUNDS, STEPS, 8, N), f32),
            dma((ROUNDS, STEPS)),
            dma((ROUNDS, 4)),
            dma((PACKS,)),
            dma((PACKS,)),
            dma((PACKS, STEPS)),
            dma((PACKS,)),
            dma((PACKS, STEPS)),
            dma((PACKS,)),
            dma((1,)),
            dma((PACKS,)),
            dma((2,)),
            dma((2,)),
        ],
        compiler_params=pltpu.CompilerParams(
            collective_id=0, has_side_effects=True, vmem_limit_bytes=48 * 2**20
        ),
        name="exchange",
    )(orbitals[0], right_fwd, left_fwd, left_inv, right_inv)
    return own[None], source


def solution(mesh):
    tables = [jnp.asarray(table) for table in matrices()]
    in_specs = (P("band", "fft", None, None),)
    out_specs = (P("band", "fft", None, None), P(None, "fft", "band", None))
    body = functools.partial(local, *tables)
    return jax.shard_map(body, mesh=mesh, in_specs=in_specs, out_specs=out_specs, check_vma=False)
```

time: 634 us -> 254 us (0.40); the launches traced: 627 us -> 254 us
  waiting for transfers between devices: 451 us -> 0 us
  Pallas kernels: 0 us -> 247 us
  matrix products: 75.1 us -> 0 us
  starting transfers between devices: 46.6 us -> 0 us
  local copies, waits for them, and re-layouts: 31.1 us -> 6.83 us
  between operations: 15 us -> 0.65 us
  other arithmetic: 8.31 us -> 0 us
    psum x1 -> x0, waiting for transfers between devices: 287 us -> none  [broadcast(): return lax.psum(kept, axis)]
    pallas_call x0 -> x1, Pallas kernels: none -> 247 us  [local(): pl.pallas_call(kernel, out_shape=(jax.ShapeDtypeStruct((SLAB, N, N), f32)...]
    reduce_scatter x1 -> x0, waiting for transfers between devices: 115 us -> none  [local(): lax.psum_scatter(jnp.stack(term_list), 'band', scatter_dimension=2, tiled...]
    dot_general x48 -> x0, matrix products: 75.1 us -> none  [the longest x12 20 us: transform_axis(): sin_real = jnp.einsum(form, real_part, sine, precision=highest)]
    all_to_all x8 -> x0, waiting for transfers between devices: 49.2 us -> none  [the longest x2 15.9 us: packed_potential(): lax.all_to_all(real_part, 'fft', split_axis=2, concat_axis=1, tiled=True)]
    all_to_all x8 -> x0, starting transfers between devices: 46.4 us -> none  [the longest x2 21.1 us: packed_potential(): lax.all_to_all(real_part, 'fft', split_axis=2, concat_axis=1, tiled=True)]
    all_to_all x8 -> x0, local copies, waits for them, and re-layouts: 10.4 us -> none  [the longest x2 3.68 us: packed_potential(): lax.all_to_all(imag_part, 'fft', split_axis=1, concat_axis=2, tiled=True)]
    add x4 -> x0, local copies, waits for them, and re-layouts: 6.36 us -> none  [the longest x2 3.18 us: transform_axis(): return (cos_real - sin_imag, cos_imag + sin_real)]
  transfers between devices with their start and end apart: 10 -> 0, of which waited for: 10 -> 0; matrix products, arithmetic and copies ran while one was open for 12% -> 0% of each run, Pallas kernels for 0% -> 0%
where the time goes in v1:
time: 254 us
  Pallas kernels  247 us (97%)
  local copies, waits for them, and re-layouts  6.83 us (3%)
    pallas_call x1, Pallas kernels, local(): pl.pallas_call(kernel, out_shape=(jax.ShapeDtypeStruct((SLAB, N, N), f32)...  247 us
    unnamed x12, local copies, waits for them, and re-layouts  6.83 us

profile of v1, /device:TPU:1, one launch (start us, length us, event | category | flops | bytes accessed | tf_op | source)
XLA Modules:
  0.0 254.2 jit_solution(4378594053231427341)
XLA Ops:
  0.6 0.0 copy-start
  0.6 1.2 copy-done
  1.9 0.0 copy-start.1
  1.9 1.0 copy-done.1
  2.9 0.0 copy-start.2
  2.9 1.0 copy-done.2
  3.8 0.0 copy-start.3
  3.8 1.0 copy-done.3
  4.8 0.0 copy-start.4
  4.8 1.0 copy-done.4
  5.8 246.7 %exchange.1 = (f32[16,128,128]{2,1,0:T(8,128)S(1)}, f32[4,16,4,128]{3,2,1,0:T(4,128)S(1)}) custom-call(f32[16,128,128]{2,1,0:T(8,128)S(1)} %bitcast.2, bf16[768,256]{1,0:T(8,128)(2,1)S(1)} %copy-done.4, bf16[256,768]{1,0:T(8,128)(2,1)S(1)} %copy-done.3, bf16[256,768]{1,0:T(8,128)(2,1)S(1)} %copy-done.2, bf16[768,256]{1,0:T(8,128)(2,1)S(1)} %copy-done.1), custom_call_target="tpu_custom_call" | custom-call | tf_op jit(solution)/shard_map/exchange/pallas_call | solution.py:368
  252.5 1.0 copy.9
  253.5 0.7 copy.10
Async XLA Ops:
  0.6 1.2 copy-start
  1.9 1.0 copy-start.1
  2.9 1.0 copy-start.2
  3.8 1.0 copy-start.3
  4.8 1.0 copy-start.4

commit v2 on v1

--- a/solution.py
+++ b/solution.py
@@ -16,6 +16,7 @@
 PACKS = 2
 ZS = 8
 CELL = 51.3
+LAG = 4
 MESH = pl.DeviceIdType.MESH
 
 
@@ -38,7 +39,7 @@
         high, low = split(matrix)
         return np.concatenate([high, high, low], axis=1)
 
-    return right(forward), left(forward.T), left(forward), right(forward.T)
+    return np.stack([right(forward), right(forward.T)]), np.stack([left(forward.T), left(forward)])
 
 
 def parts(value, axis):
@@ -61,9 +62,9 @@
 
 
 def kernel(
-    orb, right_fwd, left_fwd, left_inv, right_inv, own, out,
-    srcs, send_a, recv_b, back, recv_c, terms, summed, gathered, coulomb, folded, folded_in, final, final_in,
-    src_recv, src_send, a_recv, a_send, c_recv, c_send, t_recv, t_send, z_recv, z_send, x_sem, f_sem,
+    orb_in, rights_in, lefts_in, own, out,
+    orb, rights, lefts, srcs, send_a, recv_b, back, recv_c, terms, summed, gathered, coulomb, folded, folded_in, final, final_in,
+    in_sem, src_recv, src_send, a_recv, a_send, c_recv, c_send, t_recv, t_send, z_recv, z_send, x_recv, x_send, f_recv, f_send,
 ):
     band = lax.axis_index("band")
     me = lax.axis_index("fft")
@@ -76,6 +77,13 @@
     root = jnp.logical_and(jnp.logical_and(even, x_hi == 0), core == 0)
     lead = core == 0
 
+    loads = [
+        pltpu.make_async_copy(src, dst, in_sem.at[i])
+        for i, (src, dst) in enumerate(((orb_in, orb), (rights_in, rights), (lefts_in, lefts)))
+    ]
+    for load in loads:
+        load.start()
+
     def device(z_at, x_hi_at, core_at):
         return {"band": z_at * 4 + x_hi_at * 2 + core_at, "fft": me}
 
@@ -99,6 +107,7 @@
         signal(device(lax.rem(z + step, ZS), x_hi, core))
     signal(sibling)
     signal(across)
+    loads[0].wait()
     pl.semaphore_wait(barrier, 16)
 
     def round_of(slot):
@@ -170,6 +179,8 @@
         return carry
 
     lax.fori_loop(0, SLAB, fill_coulomb, 0)
+    for load in loads[1:]:
+        load.wait()
 
     def forward(p, j):
         r_a, r_b = round_of(2 * p), round_of(2 * p + 1)
@@ -177,10 +188,10 @@
         for i in range(2):
             o = orb[2 * j + i]
             rows.append(jnp.concatenate([o * srcs[r_a, 2 * j + i], o * srcs[r_b, 2 * j + i]], axis=1))
-        along_z = from_right(jnp.concatenate(rows, axis=0), right_fwd[...])
+        along_z = from_right(jnp.concatenate(rows, axis=0), rights[0])
         real = jnp.concatenate([along_z[:N, :N], along_z[N:, :N]], axis=1)
         imag = jnp.concatenate([along_z[:N, N:], along_z[N:, N:]], axis=1)
-        along_y = from_left(left_fwd[...], jnp.concatenate([real, imag], axis=0))
+        along_y = from_left(lefts[0], jnp.concatenate([real, imag], axis=0))
         for i in range(2):
             for part in range(2):
                 send_a[p, 2 * j + i, part] = along_y[part * N : (part + 1) * N, i * N : (i + 1) * N]
@@ -196,20 +207,32 @@
             ).start()
         pltpu.make_async_copy(block(me), recv_b.at[p, place], a_recv.at[p]).start()
 
-    def first_steps(j, carry):
-        arrive(0, j)
-        arrive(1, j)
-        forward(0, j)
-        arrive(3, j)
-        arrive(2, j)
+    behind = {0: 0, 1: jnp.where(even, LAG, 1), 3: jnp.where(even, 6, 9), 2: jnp.where(even, 12, 9)}
+
+    def relay(i):
+        for slot in (0, 1, 3, 2):
+            j = i - behind[slot]
+
+            @pl.when(jnp.logical_and(j >= 0, j < STEPS))
+            def _():
+                arrive(slot, j)
+
+    def first_steps(i, carry):
+        relay(i)
+
+        @pl.when(i >= LAG)
+        def _():
+            forward(0, i - LAG)
+
         return carry
 
-    def second_steps(j, carry):
-        forward(1, j)
+    def second_steps(i, carry):
+        relay(i)
+        forward(1, i - STEPS - LAG)
         return carry
 
-    lax.fori_loop(0, STEPS, first_steps, 0)
-    lax.fori_loop(0, STEPS, second_steps, 0)
+    lax.fori_loop(0, STEPS + LAG, first_steps, 0)
+    lax.fori_loop(STEPS + LAG, 2 * STEPS + LAG, second_steps, 0)
 
     def middle(p):
         pltpu.make_async_copy(recv_b.at[p], recv_b.at[p], a_recv.at[p]).wait()
@@ -224,10 +247,10 @@
                 jnp.concatenate([flat_in[rows(part, 2 * i), :], flat_in[rows(part, 2 * i + 1), :]], axis=1)
                 for part in range(2)
             ]
-            spectrum = from_left(left_fwd[...], jnp.concatenate(blocks, axis=0))
+            spectrum = from_left(lefts[0], jnp.concatenate(blocks, axis=0))
             weight = jnp.concatenate([coulomb[2 * i], coulomb[2 * i + 1]], axis=1)
             spectrum = spectrum * jnp.concatenate([weight, weight], axis=0)
-            result = from_left(left_inv[...], spectrum)
+            result = from_left(lefts[1], spectrum)
             for part in range(2):
                 for n in range(2):
                     flat_out[rows(part, 2 * i + n), :] = result[part * N : (part + 1) * N, n * N : (n + 1) * N]
@@ -261,12 +284,12 @@
         parts_in = [
             jnp.concatenate([recv_c[p, 2 * j, part], recv_c[p, 2 * j + 1, part]], axis=1) for part in range(2)
         ]
-        along_y = from_left(left_inv[...], jnp.concatenate(parts_in, axis=0))
+        along_y = from_left(lefts[1], jnp.concatenate(parts_in, axis=0))
         rows = [
             jnp.concatenate([along_y[:N, i * N : (i + 1) * N], along_y[N:, i * N : (i + 1) * N]], axis=1)
             for i in range(2)
         ]
-        potential = from_right(jnp.concatenate(rows, axis=0), right_inv[...])
+        potential = from_right(jnp.concatenate(rows, axis=0), rights[1])
         r_a, r_b = round_of(2 * p), round_of(2 * p + 1)
         for i in range(2):
             pot_a = potential[i * N : (i + 1) * N, :N]
@@ -293,50 +316,58 @@
         for step in (4, 3, 5, 2, 6, 1, 7):
             z_at = lax.rem(z + step, ZS)
             remote(
-                rows(z_at), gathered.at[z, pl.ds(2 * p, 2), j], z_send.at[p], z_recv.at[0], device(z_at, x_hi, core)
+                rows(z_at), gathered.at[z, pl.ds(2 * p, 2), j], z_send.at[p], z_recv.at[j], device(z_at, x_hi, core)
             ).start()
         gathered[z, pl.ds(2 * p, 2), j] = summed[p, j, :, pl.ds(pl.multiple_of(z * 16, 16), 16), :]
 
-    for p in range(PACKS):
-
-        def step_body(j, carry):
-            inverse(p, j)
-
-            @pl.when(j > 0)
-            def _():
-                spread(p, j - 1)
-
-            return carry
-
-        lax.fori_loop(0, STEPS, step_body, 0)
-        spread(p, STEPS - 1)
-
-    pltpu.make_async_copy(gathered.at[pl.ds(0, 7)], gathered.at[pl.ds(0, 7)], z_recv.at[0]).wait()
-    for r in range(ROUNDS):
-        total = gathered[0, r]
-        for z_at in range(1, ZS):
-            total = total + gathered[z_at, (r - z_at // 2) % ROUNDS]
-        folded[r] = total
-
     def half(x_hi_at):
         return pl.ds(pl.multiple_of(x_hi_at * 8, 8), 8)
 
-    cross = remote(folded.at[:, :, half(1 - x_hi), :], folded_in, x_sem.at[0], x_sem.at[1], across)
-    cross.start()
-    cross.wait()
-    final[...] = folded[:, :, half(x_hi), :] + folded_in[...]
-    last = remote(final, final_in, f_sem.at[0], f_sem.at[1], sibling)
-    last.start()
-    last.wait()
-
-    def write(j, carry):
+    def cross(j):
+        return remote(
+            folded.at[j, :, half(1 - x_hi), :], folded_in.at[j], x_send.at[0], x_recv.at[j], across
+        )
+
+    def last(j):
+        return remote(final.at[j], final_in.at[j], f_send.at[0], f_recv.at[j], sibling)
+
+    def fold(j):
+        arrived = gathered.at[pl.ds(0, 7), :, j]
+        pltpu.make_async_copy(arrived, arrived, z_recv.at[j]).wait()
         for r in range(ROUNDS):
-            mine, theirs = final[r, j], final_in[r, j]
+            total = gathered[0, r, j]
+            for z_at in range(1, ZS):
+                total = total + gathered[z_at, (r - z_at // 2) % ROUNDS, j]
+            folded[j, r] = total
+        cross(j).start()
+
+    def finish(j):
+        cross(j).wait_recv()
+        final[j] = folded[j, :, half(x_hi), :] + folded_in[j]
+        last(j).start()
+
+    def write(j):
+        last(j).wait_recv()
+        for r in range(ROUNDS):
+            mine, theirs = final[j, r], final_in[j, r]
             out[r, 2 * j + core] = jnp.where(core == 0, mine[:4], mine[4:])
             out[r, 2 * j + 1 - core] = jnp.where(core == 0, theirs[:4], theirs[4:])
+
+    def second_half(p, stages, i, carry):
+        for late, stage in stages:
+            j = i - late
+
+            @pl.when(jnp.logical_and(j >= 0, j < STEPS))
+            def _():
+                stage(j)
+
         return carry
 
-    lax.fori_loop(0, STEPS, write, 0)
+    for p in range(PACKS):
+        stages = [(0, functools.partial(inverse, p)), (1, functools.partial(spread, p))]
+        if p == PACKS - 1:
+            stages += [(3, fold), (4, finish), (5, write)]
+        lax.fori_loop(0, STEPS + stages[-1][0], functools.partial(second_half, p, stages), 0)
 
     def sent(ref, sem):
         pltpu.make_async_copy(ref, ref, sem).wait()
@@ -346,6 +377,8 @@
         sent(back.at[p, pl.ds(0, 112)], c_send.at[p])
         sent(summed.at[p], t_send.at[p])
         sent(summed.at[p, pl.ds(0, 7)], z_send.at[p])
+    sent(folded_in, x_send.at[0])
+    sent(final, f_send.at[0])
 
     @pl.when(lead)
     def _():
@@ -361,7 +394,7 @@
             sent(srcs.at[0], src_send.at[0, 3])
 
 
-def local(right_fwd, left_fwd, left_inv, right_inv, orbitals):
+def local(rights, lefts, orbitals):
     f32 = jnp.float32
     dma = pltpu.SemaphoreType.DMA
     vmem = pl.BlockSpec(memory_space=pltpu.VMEM)
@@ -371,9 +404,12 @@
             jax.ShapeDtypeStruct((SLAB, N, N), f32),
             jax.ShapeDtypeStruct((ROUNDS, SLAB, 4, N), f32),
         ),
-        in_specs=[vmem] * 5,
+        in_specs=[pl.BlockSpec(memory_space=pltpu.HBM)] * 3,
         out_specs=(vmem, vmem),
         scratch_shapes=[
+            pltpu.VMEM((SLAB, N, N), f32),
+            pltpu.VMEM(rights.shape, rights.dtype),
+            pltpu.VMEM(lefts.shape, lefts.dtype),
             pltpu.VMEM((ROUNDS, SLAB, N, N), f32),
             pltpu.VMEM((PACKS, SLAB, 2, N, N), f32),
             pltpu.VMEM((PACKS, N, 2, SLAB, N), f32),
@@ -383,10 +419,11 @@
             pltpu.VMEM((PACKS, STEPS, 2, N, N), f32),
             pltpu.VMEM((ZS, ROUNDS, STEPS, 16, N), f32),
             pltpu.VMEM((SLAB, N, N), f32),
-            pltpu.VMEM((ROUNDS, STEPS, 16, N), f32),
-            pltpu.VMEM((ROUNDS, STEPS, 8, N), f32),
-            pltpu.VMEM((ROUNDS, STEPS, 8, N), f32),
-            pltpu.VMEM((ROUNDS, STEPS, 8, N), f32),
+            pltpu.VMEM((STEPS, ROUNDS, 16, N), f32),
+            pltpu.VMEM((STEPS, ROUNDS, 8, N), f32),
+            pltpu.VMEM((STEPS, ROUNDS, 8, N), f32),
+            pltpu.VMEM((STEPS, ROUNDS, 8, N), f32),
+            dma((3,)),
             dma((ROUNDS, STEPS)),
             dma((ROUNDS, 4)),
             dma((PACKS,)),
@@ -395,16 +432,18 @@
             dma((PACKS,)),
             dma((PACKS, STEPS)),
             dma((PACKS,)),
+            dma((STEPS,)),
+            dma((PACKS,)),
+            dma((STEPS,)),
             dma((1,)),
-            dma((PACKS,)),
-            dma((2,)),
-            dma((2,)),
+            dma((STEPS,)),
+            dma((1,)),
         ],
         compiler_params=pltpu.CompilerParams(
-            collective_id=0, has_side_effects=True, vmem_limit_bytes=48 * 2**20
+            collective_id=0, has_side_effects=True, vmem_limit_bytes=56 * 2**20
         ),
         name="exchange",
-    )(orbitals[0], right_fwd, left_fwd, left_inv, right_inv)
+    )(orbitals[0], rights, lefts)
     return own[None], source
 
 

time: 254 us -> 142 us (0.56)
  Pallas kernels: 247 us -> 139 us
  local copies, waits for them, and re-layouts: 6.83 us -> 2.99 us
    pallas_call x1, Pallas kernels: 247 us -> 139 us  [local(): pl.pallas_call(kernel, out_shape=(jax.ShapeDtypeStruct((SLAB, N, N), f32)...]
    unnamed x12 -> x4, local copies, waits for them, and re-layouts: 6.83 us -> 2.99 us
where the time goes in v2:
time: 142 us
  Pallas kernels  139 us (98%)
  local copies, waits for them, and re-layouts  2.99 us (2%)
    pallas_call x1, Pallas kernels, local(): pl.pallas_call(kernel, out_shape=(jax.ShapeDtypeStruct((SLAB, N, N), f32)...  139 us
    unnamed x4, local copies, waits for them, and re-layouts  2.99 us

profile of v2, /device:TPU:1, one launch (start us, length us, event | category | flops | bytes accessed | tf_op | source)
XLA Modules:
  0.0 142.3 jit_solution(15545003146082976825)
XLA Ops:
  0.6 138.6 %exchange.1 = (f32[16,128,128]{2,1,0:T(8,128)}, f32[4,16,4,128]{3,2,1,0:T(4,128)}) custom-call(f32[16,128,128]{2,1,0:T(8,128)} %bitcast.2, bf16[2,768,256]{2,1,0:T(8,128)(2,1)} %constant.4.clone.rights_in, bf16[2,256,768]{2,1,0:T(8,128)(2,1)} %constant.5.clone.lefts_in), custom_call_target="tpu_custom_call" | custom-call | tf_op jit(solution)/shard_map/exchange/pallas_call | solution.py:401
  139.3 0.0 copy-start
  139.3 2.3 %copy.7 = f32[1,16,128,128]{3,2,1,0:T(8,128)} copy(f32[1,16,128,128]{3,2,1,0:T(8,128)} %bitcast.3) | data formatting | bytes 2097152
  141.6 0.0 copy-done
  141.6 0.7 copy.8
Async XLA Ops:
  139.3 2.3 %copy-start = (f32[4,16,4,128]{3,2,1,0:T(4,128)S(1)}, f32[4,16,4,128]{3,2,1,0:T(4,128)}, u32[]{:S(2)}) copy-start(f32[4,16,4,128]{3,2,1,0:T(4,128)} %get-tuple-element.9) | copy-start | bytes 393220

commit v3 on v2

--- a/solution.py
+++ b/solution.py
@@ -16,7 +16,9 @@
 PACKS = 2
 ZS = 8
 CELL = 51.3
-LAG = 4
+LAG = 3
+EARLY = 4
+AHEAD = 3
 MESH = pl.DeviceIdType.MESH
 
 
@@ -63,8 +65,8 @@
 
 def kernel(
     orb_in, rights_in, lefts_in, own, out,
-    orb, rights, lefts, srcs, send_a, recv_b, back, recv_c, terms, summed, gathered, coulomb, folded, folded_in, final, final_in,
-    in_sem, src_recv, src_send, a_recv, a_send, c_recv, c_send, t_recv, t_send, z_recv, z_send, x_recv, x_send, f_recv, f_send,
+    orb, rights, lefts, srcs, send_a, recv_b, back, recv_c, terms, summed, gathered, coulomb, folded, folded_in,
+    in_sem, src_recv, src_send, a_recv, a_send, c_recv, c_send, t_recv, t_send, z_recv, z_send, x_recv, x_send,
 ):
     band = lax.axis_index("band")
     me = lax.axis_index("fft")
@@ -89,6 +91,7 @@
 
     plus = device(lax.rem(z + 1, ZS), x_hi, core)
     minus = device(lax.rem(z + ZS - 1, ZS), x_hi, core)
+    minus2 = device(lax.rem(z + ZS - 2, ZS), x_hi, core)
     sibling = device(z, x_hi, 1 - core)
     across = device(z, 1 - x_hi, core)
 
@@ -107,8 +110,9 @@
         signal(device(lax.rem(z + step, ZS), x_hi, core))
     signal(sibling)
     signal(across)
+    signal(device(z, 1 - x_hi, 1 - core))
     loads[0].wait()
-    pl.semaphore_wait(barrier, 16)
+    pl.semaphore_wait(barrier, 17)
 
     def round_of(slot):
         return lax.rem(z // 2 + slot, ROUNDS)
@@ -125,14 +129,20 @@
         r = round_of(slot)
         remote(src, srcs.at[r, planes(j)], src_send.at[slot, kind], src_recv.at[r, j], target).start()
 
+    def pass_early(chunk, j):
+        @pl.when(j < EARLY)
+        def _():
+            pass_on(chunk, 0, j, 4, minus2)
+
     @pl.when(root)
     def _():
         def body(j, carry):
             chunk = orb.at[planes(j)]
+            pass_on(chunk, 0, j, 3, across)
+            pass_early(chunk, j)
+            pass_on(chunk, 0, j, 1, minus)
             pass_on(chunk, 0, j, 0, plus)
-            pass_on(chunk, 0, j, 1, minus)
             pass_on(chunk, 0, j, 2, sibling)
-            pass_on(chunk, 0, j, 3, across)
             return carry
 
         lax.fori_loop(0, STEPS, body, 0)
@@ -152,16 +162,21 @@
 
             @pl.when(lead)
             def _():
+                if slot == 1:
+
+                    @pl.when(jnp.logical_or(even, j >= EARLY))
+                    def _():
+                        pass_on(chunk, slot, j, 1, minus)
+
+                if slot == 0:
+
+                    @pl.when(even)
+                    def _():
+                        pass_early(chunk, j)
+                        pass_on(chunk, slot, j, 1, minus)
+
                 if slot in (0, 3):
                     pass_on(chunk, slot, j, 0, plus)
-                if slot == 1:
-                    pass_on(chunk, slot, j, 1, minus)
-                if slot == 0:
-
-                    @pl.when(even)
-                    def _():
-                        pass_on(chunk, slot, j, 1, minus)
-
                 pass_on(chunk, slot, j, 2, sibling)
 
         if slot == 0:
@@ -207,7 +222,7 @@
             ).start()
         pltpu.make_async_copy(block(me), recv_b.at[p, place], a_recv.at[p]).start()
 
-    behind = {0: 0, 1: jnp.where(even, LAG, 1), 3: jnp.where(even, 6, 9), 2: jnp.where(even, 12, 9)}
+    behind = {0: 0, 1: jnp.where(even, LAG, 1), 3: jnp.where(even, 6, 9), 2: jnp.where(even, 11, 9)}
 
     def relay(i):
         for slot in (0, 1, 3, 2):
@@ -230,9 +245,6 @@
         relay(i)
         forward(1, i - STEPS - LAG)
         return carry
-
-    lax.fori_loop(0, STEPS + LAG, first_steps, 0)
-    lax.fori_loop(STEPS + LAG, 2 * STEPS + LAG, second_steps, 0)
 
     def middle(p):
         pltpu.make_async_copy(recv_b.at[p], recv_b.at[p], a_recv.at[p]).wait()
@@ -258,25 +270,20 @@
 
         lax.fori_loop(0, SLAB // 2, body, 0)
 
-        def give(j, carry):
-            def place(ref):
-                return ref.at[p, planes(j), :, pl.ds(pl.multiple_of(me * SLAB, SLAB), SLAB), :]
-
-            for step in (5, 7, 6, 1, 3, 2, 4):
-                f = peer_index(step)
-                remote(
-                    back.at[p, pl.ds(f * SLAB + 2 * j, 2)], place(recv_c), c_send.at[p], c_recv.at[p, j],
-                    {"band": band, "fft": f},
-                ).start()
-            pltpu.make_async_copy(
-                back.at[p, pl.ds(me * SLAB + 2 * j, 2)], place(recv_c), c_recv.at[p, j]
+    def give(p, j, carry):
+        def place(ref):
+            return ref.at[p, planes(j), :, pl.ds(pl.multiple_of(me * SLAB, SLAB), SLAB), :]
+
+        for step in (5, 7, 6, 1, 3, 2, 4):
+            f = peer_index(step)
+            remote(
+                back.at[p, pl.ds(f * SLAB + 2 * j, 2)], place(recv_c), c_send.at[p], c_recv.at[p, j],
+                {"band": band, "fft": f},
             ).start()
-            return carry
-
-        lax.fori_loop(0, STEPS, give, 0)
-
-    for p in range(PACKS):
-        middle(p)
+        pltpu.make_async_copy(
+            back.at[p, pl.ds(me * SLAB + 2 * j, 2)], place(recv_c), c_recv.at[p, j]
+        ).start()
+        return carry
 
     def inverse(p, j):
         chunk = recv_c.at[p, planes(j)]
@@ -320,38 +327,44 @@
             ).start()
         gathered[z, pl.ds(2 * p, 2), j] = summed[p, j, :, pl.ds(pl.multiple_of(z * 16, 16), 16), :]
 
-    def half(x_hi_at):
-        return pl.ds(pl.multiple_of(x_hi_at * 8, 8), 8)
-
-    def cross(j):
+    others = (
+        (1 - x_hi, core, across), (x_hi, 1 - core, sibling), (1 - x_hi, 1 - core, device(z, 1 - x_hi, 1 - core)),
+    )
+
+    def last(j, n):
+        x_hi_at, core_at, target = others[n]
         return remote(
-            folded.at[j, :, half(1 - x_hi), :], folded_in.at[j], x_send.at[0], x_recv.at[j], across
+            folded.at[j, x_hi_at, core_at], folded_in.at[n, j], x_send.at[n], x_recv.at[n, j], target
         )
-
-    def last(j):
-        return remote(final.at[j], final_in.at[j], f_send.at[0], f_recv.at[j], sibling)
 
     def fold(j):
         arrived = gathered.at[pl.ds(0, 7), :, j]
         pltpu.make_async_copy(arrived, arrived, z_recv.at[j]).wait()
+        totals = []
         for r in range(ROUNDS):
             total = gathered[0, r, j]
             for z_at in range(1, ZS):
                 total = total + gathered[z_at, (r - z_at // 2) % ROUNDS, j]
-            folded[j, r] = total
-        cross(j).start()
-
-    def finish(j):
-        cross(j).wait_recv()
-        final[j] = folded[j, :, half(x_hi), :] + folded_in[j]
-        last(j).start()
+            totals.append(total)
+        for x_hi_at in range(2):
+            for core_at in range(2):
+                for n in range(2):
+                    rows = slice(8 * x_hi_at + 4 * core_at, 8 * x_hi_at + 4 * core_at + 4)
+                    folded[j, x_hi_at, core_at, n] = jnp.concatenate(
+                        [totals[2 * n][rows], totals[2 * n + 1][rows]], axis=0
+                    )
+        for n in range(3):
+            last(j, n).start()
 
     def write(j):
-        last(j).wait_recv()
+        for n in range(3):
+            last(j, n).wait_recv()
+        mine = folded[j, x_hi, core] + folded_in[0, j]
+        theirs = folded_in[1, j] + folded_in[2, j]
         for r in range(ROUNDS):
-            mine, theirs = final[j, r], final_in[j, r]
-            out[r, 2 * j + core] = jnp.where(core == 0, mine[:4], mine[4:])
-            out[r, 2 * j + 1 - core] = jnp.where(core == 0, theirs[:4], theirs[4:])
+            rows = slice(4 * (r % 2), 4 * (r % 2) + 4)
+            out[r, 2 * j + core] = mine[r // 2, rows]
+            out[r, 2 * j + 1 - core] = theirs[r // 2, rows]
 
     def second_half(p, stages, i, carry):
         for late, stage in stages:
@@ -363,11 +376,23 @@
 
         return carry
 
-    for p in range(PACKS):
-        stages = [(0, functools.partial(inverse, p)), (1, functools.partial(spread, p))]
-        if p == PACKS - 1:
-            stages += [(3, fold), (4, finish), (5, write)]
-        lax.fori_loop(0, STEPS + stages[-1][0], functools.partial(second_half, p, stages), 0)
+    stages = [[(0, functools.partial(inverse, p)), (1, functools.partial(spread, p))] for p in range(PACKS)]
+    stages[1] += [(3, fold), (5, write)]
+
+    def finish(p, start, stop):
+        lax.fori_loop(start, stop, functools.partial(second_half, p, stages[p]), 0)
+
+    lax.fori_loop(0, STEPS + LAG, first_steps, 0)
+    lax.fori_loop(STEPS + LAG, STEPS + LAG + AHEAD, second_steps, 0)
+    middle(0)
+    lax.fori_loop(0, STEPS - AHEAD, functools.partial(give, 0), 0)
+    lax.fori_loop(STEPS + LAG + AHEAD, 2 * STEPS + LAG, second_steps, 0)
+    lax.fori_loop(STEPS - AHEAD, STEPS, functools.partial(give, 0), 0)
+    finish(0, 0, STEPS - AHEAD)
+    middle(1)
+    lax.fori_loop(0, STEPS, functools.partial(give, 1), 0)
+    finish(0, STEPS - AHEAD, STEPS + 1)
+    finish(1, 0, STEPS + 5)
 
     def sent(ref, sem):
         pltpu.make_async_copy(ref, ref, sem).wait()
@@ -377,17 +402,23 @@
         sent(back.at[p, pl.ds(0, 112)], c_send.at[p])
         sent(summed.at[p], t_send.at[p])
         sent(summed.at[p, pl.ds(0, 7)], z_send.at[p])
-    sent(folded_in, x_send.at[0])
-    sent(final, f_send.at[0])
+    for n in range(3):
+        sent(folded_in.at[n], x_send.at[n])
 
     @pl.when(lead)
     def _():
-        for slot, kind in ((0, 0), (0, 2), (1, 1), (1, 2), (2, 2), (3, 0), (3, 2)):
+        for slot, kind in ((0, 0), (0, 2), (1, 2), (2, 2), (3, 0), (3, 2)):
             sent(srcs.at[slot], src_send.at[slot, kind])
 
         @pl.when(even)
         def _():
             sent(srcs.at[0], src_send.at[0, 1])
+            sent(srcs.at[1], src_send.at[1, 1])
+            sent(srcs.at[0, pl.ds(0, 2 * EARLY)], src_send.at[0, 4])
+
+        @pl.when(jnp.logical_not(even))
+        def _():
+            sent(srcs.at[1, pl.ds(2 * EARLY, SLAB - 2 * EARLY)], src_send.at[1, 1])
 
         @pl.when(root)
         def _():
@@ -419,13 +450,11 @@
             pltpu.VMEM((PACKS, STEPS, 2, N, N), f32),
             pltpu.VMEM((ZS, ROUNDS, STEPS, 16, N), f32),
             pltpu.VMEM((SLAB, N, N), f32),
-            pltpu.VMEM((STEPS, ROUNDS, 16, N), f32),
-            pltpu.VMEM((STEPS, ROUNDS, 8, N), f32),
-            pltpu.VMEM((STEPS, ROUNDS, 8, N), f32),
-            pltpu.VMEM((STEPS, ROUNDS, 8, N), f32),
+            pltpu.VMEM((STEPS, 2, 2, 2, 8, N), f32),
+            pltpu.VMEM((3, STEPS, 2, 8, N), f32),
             dma((3,)),
             dma((ROUNDS, STEPS)),
-            dma((ROUNDS, 4)),
+            dma((ROUNDS, 5)),
             dma((PACKS,)),
             dma((PACKS,)),
             dma((PACKS, STEPS)),
@@ -434,10 +463,8 @@
             dma((PACKS,)),
             dma((STEPS,)),
             dma((PACKS,)),
-            dma((STEPS,)),
-            dma((1,)),
-            dma((STEPS,)),
-            dma((1,)),
+            dma((3, STEPS)),
+            dma((3,)),
         ],
         compiler_params=pltpu.CompilerParams(
             collective_id=0, has_side_effects=True, vmem_limit_bytes=56 * 2**20

time: 142 us -> 145 us (1.021)
  Pallas kernels: 139 us -> 141 us
    pallas_call x1, Pallas kernels: 139 us -> 141 us  [local(): pl.pallas_call(kernel, out_shape=(jax.ShapeDtypeStruct((SLAB, N, N), f32)...]
where the time goes in v3:
time: 145 us
  Pallas kernels  141 us (97%)
  local copies, waits for them, and re-layouts  2.99 us (2%)
    pallas_call x1, Pallas kernels, local(): pl.pallas_call(kernel, out_shape=(jax.ShapeDtypeStruct((SLAB, N, N), f32)...  141 us
    unnamed x4, local copies, waits for them, and re-layouts  2.99 us

profile of v3, /device:TPU:1, one launch (start us, length us, event | category | flops | bytes accessed | tf_op | source)
XLA Modules:
  0.0 144.9 jit_solution(8917442994260378476)
XLA Ops:
  0.6 141.3 %exchange.1 = (f32[16,128,128]{2,1,0:T(8,128)}, f32[4,16,4,128]{3,2,1,0:T(4,128)}) custom-call(f32[16,128,128]{2,1,0:T(8,128)} %bitcast.2, bf16[2,768,256]{2,1,0:T(8,128)(2,1)} %constant.4.clone.rights_in, bf16[2,256,768]{2,1,0:T(8,128)(2,1)} %constant.5.clone.lefts_in), custom_call_target="tpu_custom_call" | custom-call | tf_op jit(solution)/shard_map/exchange/pallas_call | solution.py:432
  141.9 0.0 copy-start
  141.9 2.3 %copy.7 = f32[1,16,128,128]{3,2,1,0:T(8,128)} copy(f32[1,16,128,128]{3,2,1,0:T(8,128)} %bitcast.3) | data formatting | bytes 2097152
  144.3 0.0 copy-done
  144.3 0.7 copy.8
Async XLA Ops:
  141.9 2.3 %copy-start = (f32[4,16,4,128]{3,2,1,0:T(4,128)S(1)}, f32[4,16,4,128]{3,2,1,0:T(4,128)}, u32[]{:S(2)}) copy-start(f32[4,16,4,128]{3,2,1,0:T(4,128)} %get-tuple-element.9) | copy-start | bytes 393220

commit v4 on v3

--- a/solution.py
+++ b/solution.py
@@ -18,7 +18,6 @@
 CELL = 51.3
 LAG = 3
 EARLY = 4
-AHEAD = 3
 MESH = pl.DeviceIdType.MESH
 
 
@@ -134,18 +133,18 @@
         def _():
             pass_on(chunk, 0, j, 4, minus2)
 
+    def pass_own(j):
+        chunk = orb.at[planes(j)]
+        pass_on(chunk, 0, j, 3, across)
+        pass_early(chunk, j)
+        pass_on(chunk, 0, j, 1, minus)
+        pass_on(chunk, 0, j, 0, plus)
+        pass_on(chunk, 0, j, 2, sibling)
+
     @pl.when(root)
     def _():
-        def body(j, carry):
-            chunk = orb.at[planes(j)]
-            pass_on(chunk, 0, j, 3, across)
-            pass_early(chunk, j)
-            pass_on(chunk, 0, j, 1, minus)
-            pass_on(chunk, 0, j, 0, plus)
-            pass_on(chunk, 0, j, 2, sibling)
-            return carry
-
-        lax.fori_loop(0, STEPS, body, 0)
+        for j in range(LAG):
+            pass_own(j)
 
         def fill(j, carry):
             srcs[round_of(0), planes(j)] = orb[planes(j)]
@@ -233,6 +232,10 @@
                 arrive(slot, j)
 
     def first_steps(i, carry):
+        @pl.when(jnp.logical_and(root, jnp.logical_and(i >= LAG, i < STEPS)))
+        def _():
+            pass_own(i)
+
         relay(i)
 
         @pl.when(i >= LAG)
@@ -245,6 +248,9 @@
         relay(i)
         forward(1, i - STEPS - LAG)
         return carry
+
+    lax.fori_loop(0, STEPS + LAG, first_steps, 0)
+    lax.fori_loop(STEPS + LAG, 2 * STEPS + LAG, second_steps, 0)
 
     def middle(p):
         pltpu.make_async_copy(recv_b.at[p], recv_b.at[p], a_recv.at[p]).wait()
@@ -270,20 +276,25 @@
 
         lax.fori_loop(0, SLAB // 2, body, 0)
 
-    def give(p, j, carry):
-        def place(ref):
-            return ref.at[p, planes(j), :, pl.ds(pl.multiple_of(me * SLAB, SLAB), SLAB), :]
-
-        for step in (5, 7, 6, 1, 3, 2, 4):
-            f = peer_index(step)
-            remote(
-                back.at[p, pl.ds(f * SLAB + 2 * j, 2)], place(recv_c), c_send.at[p], c_recv.at[p, j],
-                {"band": band, "fft": f},
+        def give(j, carry):
+            def place(ref):
+                return ref.at[p, planes(j), :, pl.ds(pl.multiple_of(me * SLAB, SLAB), SLAB), :]
+
+            for step in (5, 7, 6, 1, 3, 2, 4):
+                f = peer_index(step)
+                remote(
+                    back.at[p, pl.ds(f * SLAB + 2 * j, 2)], place(recv_c), c_send.at[p], c_recv.at[p, j],
+                    {"band": band, "fft": f},
+                ).start()
+            pltpu.make_async_copy(
+                back.at[p, pl.ds(me * SLAB + 2 * j, 2)], place(recv_c), c_recv.at[p, j]
             ).start()
-        pltpu.make_async_copy(
-            back.at[p, pl.ds(me * SLAB + 2 * j, 2)], place(recv_c), c_recv.at[p, j]
-        ).start()
-        return carry
+            return carry
+
+        lax.fori_loop(0, STEPS, give, 0)
+
+    for p in range(PACKS):
+        middle(p)
 
     def inverse(p, j):
         chunk = recv_c.at[p, planes(j)]
@@ -376,23 +387,11 @@
 
         return carry
 
-    stages = [[(0, functools.partial(inverse, p)), (1, functools.partial(spread, p))] for p in range(PACKS)]
-    stages[1] += [(3, fold), (5, write)]
-
-    def finish(p, start, stop):
-        lax.fori_loop(start, stop, functools.partial(second_half, p, stages[p]), 0)
-
-    lax.fori_loop(0, STEPS + LAG, first_steps, 0)
-    lax.fori_loop(STEPS + LAG, STEPS + LAG + AHEAD, second_steps, 0)
-    middle(0)
-    lax.fori_loop(0, STEPS - AHEAD, functools.partial(give, 0), 0)
-    lax.fori_loop(STEPS + LAG + AHEAD, 2 * STEPS + LAG, second_steps, 0)
-    lax.fori_loop(STEPS - AHEAD, STEPS, functools.partial(give, 0), 0)
-    finish(0, 0, STEPS - AHEAD)
-    middle(1)
-    lax.fori_loop(0, STEPS, functools.partial(give, 1), 0)
-    finish(0, STEPS - AHEAD, STEPS + 1)
-    finish(1, 0, STEPS + 5)
+    for p in range(PACKS):
+        stages = [(0, functools.partial(inverse, p)), (1, functools.partial(spread, p))]
+        if p == PACKS - 1:
+            stages += [(3, fold), (5, write)]
+        lax.fori_loop(0, STEPS + stages[-1][0], functools.partial(second_half, p, stages), 0)
 
     def sent(ref, sem):
         pltpu.make_async_copy(ref, ref, sem).wait()

time: 145 us -> 144 us (level)
  no operation moved by 1% of the time
where the time goes in v4:
time: 144 us
  Pallas kernels  140 us (97%)
  local copies, waits for them, and re-layouts  2.99 us (2%)
    pallas_call x1, Pallas kernels, local(): pl.pallas_call(kernel, out_shape=(jax.ShapeDtypeStruct((SLAB, N, N), f32)...  140 us
    unnamed x4, local copies, waits for them, and re-layouts  2.99 us

profile of v4, /device:TPU:1, one launch (start us, length us, event | category | flops | bytes accessed | tf_op | source)
XLA Modules:
  0.0 144.1 jit_solution(3164506554724509309)
XLA Ops:
  0.6 140.4 %exchange.1 = (f32[16,128,128]{2,1,0:T(8,128)}, f32[4,16,4,128]{3,2,1,0:T(4,128)}) custom-call(f32[16,128,128]{2,1,0:T(8,128)} %bitcast.2, bf16[2,768,256]{2,1,0:T(8,128)(2,1)} %constant.4.clone.rights_in, bf16[2,256,768]{2,1,0:T(8,128)(2,1)} %constant.5.clone.lefts_in), custom_call_target="tpu_custom_call" | custom-call | tf_op jit(solution)/shard_map/exchange/pallas_call | solution.py:431
  141.1 0.0 copy-start
  141.1 2.3 %copy.7 = f32[1,16,128,128]{3,2,1,0:T(8,128)} copy(f32[1,16,128,128]{3,2,1,0:T(8,128)} %bitcast.3) | data formatting | bytes 2097152
  143.4 0.0 copy-done
  143.4 0.7 copy.8
Async XLA Ops:
  141.1 2.3 %copy-start = (f32[4,16,4,128]{3,2,1,0:T(4,128)S(1)}, f32[4,16,4,128]{3,2,1,0:T(4,128)}, u32[]{:S(2)}) copy-start(f32[4,16,4,128]{3,2,1,0:T(4,128)} %get-tuple-element.9) | copy-start | bytes 393220

commit v5 on v4

--- a/solution.py
+++ b/solution.py
@@ -13,6 +13,7 @@
 ROUNDS = 4
 SLAB = 16
 STEPS = 8
+DEPTH = 2
 PACKS = 2
 ZS = 8
 CELL = 51.3
@@ -133,18 +134,18 @@
         def _():
             pass_on(chunk, 0, j, 4, minus2)
 
-    def pass_own(j):
-        chunk = orb.at[planes(j)]
-        pass_on(chunk, 0, j, 3, across)
-        pass_early(chunk, j)
-        pass_on(chunk, 0, j, 1, minus)
-        pass_on(chunk, 0, j, 0, plus)
-        pass_on(chunk, 0, j, 2, sibling)
-
     @pl.when(root)
     def _():
-        for j in range(LAG):
-            pass_own(j)
+        def body(j, carry):
+            chunk = orb.at[planes(j)]
+            pass_on(chunk, 0, j, 3, across)
+            pass_early(chunk, j)
+            pass_on(chunk, 0, j, 1, minus)
+            pass_on(chunk, 0, j, 0, plus)
+            pass_on(chunk, 0, j, 2, sibling)
+            return carry
+
+        lax.fori_loop(0, STEPS, body, 0)
 
         def fill(j, carry):
             srcs[round_of(0), planes(j)] = orb[planes(j)]
@@ -195,6 +196,10 @@
     lax.fori_loop(0, SLAB, fill_coulomb, 0)
     for load in loads[1:]:
         load.wait()
+
+    def left_fwd(p, j):
+        blocks = send_a.at[p, pl.ds(0, 2), :, pl.ds(0, 7 * SLAB), :]
+        pltpu.make_async_copy(blocks, blocks, a_send.at[p, j]).wait()
 
     def forward(p, j):
         r_a, r_b = round_of(2 * p), round_of(2 * p + 1)
@@ -214,10 +219,14 @@
         def block(f):
             return send_a.at[p, planes(j), :, pl.ds(pl.multiple_of(f * SLAB, SLAB), SLAB), :]
 
+        if p > 0:
+            pl.when(j < DEPTH)(lambda: left_fwd(p - 1, j + STEPS - DEPTH))
+        pl.when(j >= DEPTH)(lambda: left_fwd(p, j - DEPTH))
+
         for step in (5, 7, 6, 1, 3, 2, 4):
             f = peer_index(step)
             remote(
-                block(f), recv_b.at[p, place], a_send.at[p], a_recv.at[p], {"band": band, "fft": f}
+                block(f), recv_b.at[p, place], a_send.at[p, j], a_recv.at[p], {"band": band, "fft": f}
             ).start()
         pltpu.make_async_copy(block(me), recv_b.at[p, place], a_recv.at[p]).start()
 
@@ -232,10 +241,6 @@
                 arrive(slot, j)
 
     def first_steps(i, carry):
-        @pl.when(jnp.logical_and(root, jnp.logical_and(i >= LAG, i < STEPS)))
-        def _():
-            pass_own(i)
-
         relay(i)
 
         @pl.when(i >= LAG)
@@ -393,11 +398,13 @@
             stages += [(3, fold), (5, write)]
         lax.fori_loop(0, STEPS + stages[-1][0], functools.partial(second_half, p, stages), 0)
 
+    for j in range(STEPS - DEPTH, STEPS):
+        left_fwd(PACKS - 1, j)
+
     def sent(ref, sem):
         pltpu.make_async_copy(ref, ref, sem).wait()
 
     for p in range(PACKS):
-        sent(send_a.at[p, pl.ds(0, 14)], a_send.at[p])
         sent(back.at[p, pl.ds(0, 112)], c_send.at[p])
         sent(summed.at[p], t_send.at[p])
         sent(summed.at[p, pl.ds(0, 7)], z_send.at[p])
@@ -455,7 +462,7 @@
             dma((ROUNDS, STEPS)),
             dma((ROUNDS, 5)),
             dma((PACKS,)),
-            dma((PACKS,)),
+            dma((PACKS, STEPS)),
             dma((PACKS, STEPS)),
             dma((PACKS,)),
             dma((PACKS, STEPS)),

time: 144 us -> 142 us (0.986)
  Pallas kernels: 140 us -> 138 us
    pallas_call x1, Pallas kernels: 140 us -> 138 us  [local(): pl.pallas_call(kernel, out_shape=(jax.ShapeDtypeStruct((SLAB, N, N), f32)...]
where the time goes in v5:
time: 142 us; the launch traced here: 141 us
  Pallas kernels  138 us (97%)
  local copies, waits for them, and re-layouts  2.99 us (2%)
    pallas_call x1, Pallas kernels, local(): pl.pallas_call(kernel, out_shape=(jax.ShapeDtypeStruct((SLAB, N, N), f32)...  138 us
    unnamed x4, local copies, waits for them, and re-layouts  2.99 us

profile of v5, /device:TPU:1, one launch (start us, length us, event | category | flops | bytes accessed | tf_op | source)
XLA Modules:
  0.0 141.4 jit_solution(15882899301852169807)
XLA Ops:
  0.6 137.8 %exchange.1 = (f32[16,128,128]{2,1,0:T(8,128)}, f32[4,16,4,128]{3,2,1,0:T(4,128)}) custom-call(f32[16,128,128]{2,1,0:T(8,128)} %bitcast.2, bf16[2,768,256]{2,1,0:T(8,128)(2,1)} %constant.4.clone.rights_in, bf16[2,256,768]{2,1,0:T(8,128)(2,1)} %constant.5.clone.lefts_in), custom_call_target="tpu_custom_call" | custom-call | tf_op jit(solution)/shard_map/exchange/pallas_call | solution.py:438
  138.4 0.0 copy-start
  138.4 2.3 %copy.7 = f32[1,16,128,128]{3,2,1,0:T(8,128)} copy(f32[1,16,128,128]{3,2,1,0:T(8,128)} %bitcast.3) | data formatting | bytes 2097152
  140.8 0.0 copy-done
  140.8 0.7 copy.8
Async XLA Ops:
  138.4 2.3 %copy-start = (f32[4,16,4,128]{3,2,1,0:T(4,128)S(1)}, f32[4,16,4,128]{3,2,1,0:T(4,128)}, u32[]{:S(2)}) copy-start(f32[4,16,4,128]{3,2,1,0:T(4,128)} %get-tuple-element.9) | copy-start | bytes 393220

commit v6 on v5

--- a/solution.py
+++ b/solution.py
@@ -111,6 +111,17 @@
     signal(sibling)
     signal(across)
     signal(device(z, 1 - x_hi, 1 - core))
+    def fill_coulomb(k, carry):
+        row = lax.broadcasted_iota(jnp.int32, (N, N), 0)
+        column = lax.broadcasted_iota(jnp.int32, (N, N), 1)
+        middle = jnp.full((N, N), me * SLAB + k, jnp.int32)
+        total = signed_square(row) + signed_square(middle) + signed_square(column)
+        scale = CELL * CELL / np.pi / float(N) ** 3
+        coulomb[k] = jnp.where(total > 0, scale / jnp.maximum(total, 1.0), 0.0)
+        return carry
+
+    lax.fori_loop(0, SLAB, fill_coulomb, 0)
+
     loads[0].wait()
     pl.semaphore_wait(barrier, 17)
 
@@ -184,16 +195,6 @@
         else:
             take()
 
-    def fill_coulomb(k, carry):
-        row = lax.broadcasted_iota(jnp.int32, (N, N), 0)
-        column = lax.broadcasted_iota(jnp.int32, (N, N), 1)
-        middle = jnp.full((N, N), me * SLAB + k, jnp.int32)
-        total = signed_square(row) + signed_square(middle) + signed_square(column)
-        scale = CELL * CELL / np.pi / float(N) ** 3
-        coulomb[k] = jnp.where(total > 0, scale / jnp.maximum(total, 1.0), 0.0)
-        return carry
-
-    lax.fori_loop(0, SLAB, fill_coulomb, 0)
     for load in loads[1:]:
         load.wait()
 

time: 142 us -> 142 us (level)
  no operation moved by 1% of the time
where the time goes in v6:
time: 142 us; the launch traced here: 141 us
  Pallas kernels  138 us (97%)
  local copies, waits for them, and re-layouts  2.99 us (2%)
    pallas_call x1, Pallas kernels, local(): pl.pallas_call(kernel, out_shape=(jax.ShapeDtypeStruct((SLAB, N, N), f32)...  138 us
    unnamed x4, local copies, waits for them, and re-layouts  2.99 us

profile of v6, /device:TPU:1, one launch (start us, length us, event | category | flops | bytes accessed | tf_op | source)
XLA Modules:
  0.0 141.4 jit_solution(2557890647350660083)
XLA Ops:
  0.6 137.8 %exchange.1 = (f32[16,128,128]{2,1,0:T(8,128)}, f32[4,16,4,128]{3,2,1,0:T(4,128)}) custom-call(f32[16,128,128]{2,1,0:T(8,128)} %bitcast.2, bf16[2,768,256]{2,1,0:T(8,128)(2,1)} %constant.4.clone.rights_in, bf16[2,256,768]{2,1,0:T(8,128)(2,1)} %constant.5.clone.lefts_in), custom_call_target="tpu_custom_call" | custom-call | tf_op jit(solution)/shard_map/exchange/pallas_call | solution.py:439
  138.4 0.0 copy-start
  138.4 2.3 %copy.7 = f32[1,16,128,128]{3,2,1,0:T(8,128)} copy(f32[1,16,128,128]{3,2,1,0:T(8,128)} %bitcast.3) | data formatting | bytes 2097152
  140.8 0.0 copy-done
  140.8 0.7 copy.8
Async XLA Ops:
  138.4 2.3 %copy-start = (f32[4,16,4,128]{3,2,1,0:T(4,128)S(1)}, f32[4,16,4,128]{3,2,1,0:T(4,128)}, u32[]{:S(2)}) copy-start(f32[4,16,4,128]{3,2,1,0:T(4,128)} %get-tuple-element.9) | copy-start | bytes 393220
